TPU v7x, 32 devices: a whole 2x2x4 slice. The times are simulated.
32 devices in a mesh: col: 16 (over z, y, x), row: 2 (over core).
Axes of the slice: x: 2, y: 2, z: 4, core: 2. Of those that a mesh axis runs over, the one named last changes fastest.
Arguments:
- k_blocks: bfloat16 [2, 16, 4, 256, 256], P('row', 'col'), may hold values from -0.1875 to 0.1875
- slot_row: int32 [2, 16, 4], P('row', 'col'), may hold values from 0 to 3
- slot_col: int32 [2, 16, 4], P('row', 'col'), may hold values from 0 to 3
- live_count: int32 [2, 16], P('row', 'col'), may hold values from 1 to 4, as said below
- cost: float32 [16384], P('col'), may hold values from -6 to 6
- upper: float32 [16384], P('col'), may hold values from 0.5 to 2
- tau: float32 [16384], P('col'), may hold values from 0.2 to 0.8
- sigma: float32 [2, 1024], P('row', 'col'), may hold values from 0.2 to 0.8
- demand: float32 [2, 1024, 128], P('row', 'col'), may hold values from -6 to 6
- primal_start: float32 [16384, 128], P('col'), may hold values from 0 to 1
- dual_start: float32 [2, 1024, 128], P('row', 'col'), may hold values from 0 to 1
Outputs:
- primal: float32 [16384, 128], P('col')
- dual: float32 [2, 1024, 128], P('row', 'col')
Inputs may be any that keep to these rules, and one draw needn't show every extreme that they name: `live_count`: only slots below a device's count belong to K; the blocks in later slots are ignored. Some device has all 4 slots in use.
All inputs are finite; a program needn't handle non-finite values.
Results may differ from a plain program's by a relative error of at most 0.0023.
Values may be sent and summed in bfloat16 or wider, within the bound.
A program may use at most 64 MiB of HBM per device.

v0:
```python
import jax
import jax.numpy as jnp
from jax import lax
from jax.sharding import PartitionSpec as P

ITERS = 2


def transpose_terms(blocks, row_hot, col_hot, everyone):
    chosen = jnp.einsum(
        "kg,gis->kis", row_hot.astype(jnp.bfloat16), everyone, preferred_element_type=jnp.float32
    ).astype(jnp.bfloat16)
    terms = jnp.einsum("kij,kis->kjs", blocks, chosen, preferred_element_type=jnp.float32)
    return jnp.einsum(
        "kc,kjs->cjs", col_hot.astype(jnp.float32), terms, precision=lax.Precision.HIGHEST
    )


def forward_terms(blocks, row_hot, col_hot, extrapolated):
    chosen = jnp.einsum(
        "kc,cjs->kjs",
        col_hot.astype(jnp.bfloat16),
        extrapolated,
        preferred_element_type=jnp.float32,
    ).astype(jnp.bfloat16)
    terms = jnp.einsum("kij,kjs->kis", blocks, chosen, preferred_element_type=jnp.float32)
    return jnp.einsum(
        "kg,kis->gis", row_hot.astype(jnp.float32), terms, precision=lax.Precision.HIGHEST
    )


def on_device(
    k_blocks,
    slot_row,
    slot_col,
    live_count,
    cost,
    upper,
    tau,
    sigma,
    demand,
    primal_start,
    dual_start,
):
    blocks = k_blocks[0, 0]
    rows_of = slot_row[0, 0]
    cols_of = slot_col[0, 0]
    count = live_count[0, 0]
    slots = blocks.shape[0]
    width = blocks.shape[1]
    col_count = lax.axis_size("col")
    groups = col_count // 4
    scenarios = primal_start.shape[1]
    col_blocks = primal_start.shape[0] // width
    live = jnp.arange(slots) < count
    row_hot = (rows_of[:, None] == jnp.arange(groups)[None, :]) & live[:, None]
    col_hot = (cols_of[:, None] == jnp.arange(col_blocks)[None, :]) & live[:, None]
    primal = primal_start
    dual = dual_start[0]
    rates = sigma[0][:, None]
    needed = demand[0]
    for step in range(ITERS):
        everyone = lax.all_gather(dual.astype(jnp.bfloat16), "col", axis=0, tiled=True).reshape(
            groups, width, scenarios
        )
        per_col = transpose_terms(blocks, row_hot, col_hot, everyone)
        flat = per_col.reshape(col_blocks * width, scenarios)
        back = lax.psum(flat, "row")
        new_primal = jnp.minimum(
            jnp.maximum(primal - tau[:, None] * (cost[:, None] - back), 0.0), upper[:, None]
        )
        extrapolated = (
            (2.0 * new_primal - primal).astype(jnp.bfloat16).reshape(col_blocks, width, scenarios)
        )
        per_row = forward_terms(blocks, row_hot, col_hot, extrapolated)
        outgoing = per_row.reshape(col_count, -1, scenarios)
        incoming = lax.all_to_all(outgoing, "col", split_axis=0, concat_axis=0, tiled=True)
        forward = jnp.sum(incoming, axis=0)
        dual = jnp.maximum(dual + rates * (needed - forward), 0.0)
        primal = new_primal
    return (primal, dual[None])


def solution(mesh):
    in_specs = (
        P("row", "col", None, None, None),
        P("row", "col", None),
        P("row", "col", None),
        P("row", "col"),
        P("col"),
        P("col"),
        P("col"),
        P("row", "col"),
        P("row", "col", None),
        P("col", None),
        P("row", "col", None),
    )
    out_specs = (P("col", None), P("row", "col", None))
    return jax.shard_map(
        on_device, mesh=mesh, in_specs=in_specs, out_specs=out_specs, check_vma=False
    )
```

profile of v0, /device:TPU:0, one launch (start us, length us, event | category | flops | bytes accessed | tf_op | source)
XLA Modules:
  0.0 186.3 jit_solution(3237687826428789127)
XLA Ops:
  7.9 0.8 bitcast_convert_fusion
  8.7 43.8 %all_gather.6 = bf16[1024,128]{1,0:T(8,128)(2,1)S(1)} all-gather(bf16[64,128]{1,0:T(8,128)(2,1)S(1)} %bitcast_convert_fusion), channel_id=1, replica_groups=mesh['col'=16,'row'=2] {'col'}, dimensions={0}, use_global_device_ids=true | all-gather | bytes 278528 | tf_op jit(solution)/shard_map/all_gather | solution.py:63
  52.5 0.7 copy-done.9
  53.1 0.4 fusion.22
  53.5 0.3 fusion.14
  53.8 0.2 copy.19
  54.0 0.6 fusion.6
  54.6 0.8 copy.13
  55.5 0.0 all-reduce.5.cloned.1.call-start
  55.6 14.7 %all-reduce.3.cloned.1.call-done = f32[1024,128]{1,0:T(8,128)} async-done(((f32[1024,128]{1,0:T(8,128)}), f32[1024,128]{1,0:T(8,128)}) %all-reduce.3.cloned.1.call-update) | async-done | bytes 524304 | tf_op jit(solution)/shard_map/psum | solution.py:68
  70.3 1.5 subtract_convert_fusion.1
  71.8 0.4 fusion.20
  72.2 0.3 fusion.12
  72.5 0.2 copy.22
  72.7 0.6 fusion.4
  73.4 22.1 %all_to_all.10 = f32[16,64,128]{2,1,0:T(8,128)S(1)} all-to-all(f32[16,64,128]{2,1,0:T(8,128)S(1)} %bitcast.79), channel_id=1, replica_groups=mesh['col'=16,'row'=2] {'col'}, dimensions={0} | all-to-all | bytes 1048576 | tf_op jit(solution)/shard_map/all_to_all | solution.py:77
  95.5 0.7 copy-done.3
  96.2 0.1 fusion.33
  96.3 39.5 %all_gather.7 = bf16[1024,128]{1,0:T(8,128)(2,1)S(1)} all-gather(bf16[64,128]{1,0:T(8,128)(2,1)S(1)} %fusion.33), channel_id=1, replica_groups=mesh['col'=16,'row'=2] {'col'}, dimensions={0}, use_global_device_ids=true | all-gather | bytes 278528 | tf_op jit(solution)/shard_map/all_gather | solution.py:63
  135.7 0.4 fusion.18
  136.1 0.3 fusion.10
  136.4 0.2 copy.25
  136.6 0.6 fusion.2
  137.2 0.8 copy.15
  138.1 14.8 %all-reduce.5.cloned.1.call-done = f32[1024,128]{1,0:T(8,128)} async-done(((f32[1024,128]{1,0:T(8,128)}), f32[1024,128]{1,0:T(8,128)}) %all-reduce.5.cloned.1.call-update) | async-done | bytes 524304 | tf_op jit(solution)/shard_map/psum | solution.py:68
  152.8 2.3 %subtract_convert_fusion = (bf16[1024,128]{1,0:T(8,128)(2,1)S(1)}, f32[1024,128]{1,0:T(8,128)}) fusion(f32[1024]{0:T(1024)S(1)} %copy-done.5, f32[1024,128]{1,0:T(8,128)S(1)} %copy-done.1, f32[1024,128]{1,0:T(8,128)S(1)} %copy-done.2, f32[1024]{0:T(1024)S(1)} %copy-done.6, f32[1024]{0:T(1024)S(1)} %copy-done.7, f32[1024,128]{1,0:T(8,128)} %all-reduce.5.cloned.1.call-done), kind=kLoop, calls=%fused_computation.20 | loop fusion | flops 1703936 | bytes 2371584 | tf_op jit(solution)/shard_map/convert_element_type | solution.py:73
  155.1 0.4 fusion.16
  155.5 0.3 fusion.8
  155.8 0.2 copy.28
  156.1 0.6 fusion
  156.7 22.1 %all_to_all.11 = f32[16,64,128]{2,1,0:T(8,128)S(1)} all-to-all(f32[16,64,128]{2,1,0:T(8,128)S(1)} %bitcast.80), channel_id=1, replica_groups=mesh['col'=16,'row'=2] {'col'}, dimensions={0} | all-to-all | bytes 1048576 | tf_op jit(solution)/shard_map/all_to_all | solution.py:77
  178.8 0.7 fusion.26
  (29 shorter events, 0.3 us)
Async XLA Ops:
  7.2 46.3 %copy-start = (bf16[1,1,4,256,256]{4,3,2,1,0:T(8,128)(2,1)S(1)}, bf16[1,1,4,256,256]{4,3,2,1,0:T(8,128)(2,1)}, u32[]{:S(2)}) copy-start(bf16[1,1,4,256,256]{4,3,2,1,0:T(8,128)(2,1)} %param.11) | copy-start | bytes 1572868
  7.2 63.1 %all-reduce.3.cloned.1.call-start = ((), (), s32[]{:S(2)}) async-start(), calls=%async_computation.2 | async-start | bytes 1048576 | tf_op jit(solution)/shard_map/psum | solution.py:68
  52.5 0.7 copy-start.9
  52.5 0.7 copy-start.10
  54.6 15.6 %copy-start.6 = (f32[1024]{0:T(1024)S(1)}, f32[1024]{0:T(1024)}, u32[]{:S(2)}) copy-start(f32[1024]{0:T(1024)} %param.15) | copy-start | bytes 12292
  54.6 15.6 %copy-start.7 = (f32[1024]{0:T(1024)S(1)}, f32[1024]{0:T(1024)}, u32[]{:S(2)}) copy-start(f32[1024]{0:T(1024)} %param.17) | copy-start | bytes 12292
  55.5 14.8 %copy-start.1 = (f32[1024,128]{1,0:T(8,128)S(1)}, f32[1024,128]{1,0:T(8,128)}, u32[]{:S(2)}) copy-start(f32[1024,128]{1,0:T(8,128)} %param.20) | copy-start | bytes 1572868
  55.5 14.8 %copy-start.5 = (f32[1024]{0:T(1024)S(1)}, f32[1024]{0:T(1024)}, u32[]{:S(2)}) copy-start(f32[1024]{0:T(1024)} %param.16) | copy-start | bytes 12292
  55.5 97.3 %all-reduce.5.cloned.1.call-start = ((), (), s32[]{:S(2)}) async-start(), calls=%async_computation.3 | async-start | bytes 1048576 | tf_op jit(solution)/shard_map/psum | solution.py:68
  95.4 0.8 copy-start.3
  95.4 0.8 copy-start.4
  95.5 0.7 copy-start.8
  138.0 14.8 %copy-start.2 = (f32[1024,128]{1,0:T(8,128)S(1)}, f32[1024,128]{1,0:T(8,128)}, u32[]{:S(2)}) copy-start(f32[1024,128]{1,0:T(8,128)} %all-reduce.3.cloned.1.call-done) | copy-start | bytes 1572868
Sparse Core Ops, SparseCore 0:
  55.6 14.5 all-reduce.2
  138.2 14.5 all-reduce.4
where the time goes:
time: 187 us; the launch traced here: 186 us
  blocking collectives  127 us (68%)
  waiting for transfers between devices  29.5 us (16%)
  between operations  14.9 us (8%)
  other arithmetic  5.45 us (3%)
  matrix products  4.98 us (3%)
  local copies, waits for them, and re-layouts  4.08 us (2%)
    all_gather x2, blocking collectives, on_device(): lax.all_gather(dual.astype(jnp.bfloat16), 'col', axis=0, tiled=True)  83.2 us
    all_to_all x2, blocking collectives, on_device(): lax.all_to_all(outgoing, 'col', split_axis=0, concat_axis=0, tiled=True)  44.1 us
    psum x2, waiting for transfers between devices, on_device(): back = lax.psum(flat, 'row')  29.5 us
    convert_element_type x2, other arithmetic, on_device(): (2.0 * new_primal - primal).astype(jnp.bfloat16)  3.83 us
  transfers between devices with their start and end apart: 2, of which 2 were waited for; matrix products, arithmetic and copies ran while one was open for 0% of the time, Pallas kernels for 0%

commit v1 on v0

--- a/solution.py
+++ b/solution.py
@@ -4,6 +4,27 @@
 from jax.sharding import PartitionSpec as P
 
 ITERS = 2
+
+
+def laid_out(parts, dim):
+    parts = jnp.moveaxis(parts, 0, dim)
+    dims = parts.shape
+    return parts.reshape(*dims[:dim], dims[dim] * dims[dim + 1], *dims[dim + 2 :])
+
+
+def grow_blocks(x, axis):
+    peers, index = (lax.axis_size(axis), lax.axis_index(axis))
+    pieces, bit = (x[None], 1)
+    while bit < peers:
+        other = lax.ppermute(pieces, axis, [(i, i ^ bit) for i in range(peers)])
+        low = index & bit == 0
+        pieces = jnp.concatenate([jnp.where(low, pieces, other), jnp.where(low, other, pieces)])
+        bit *= 2
+    return pieces
+
+
+def gather_by_bits(value, axis, dim):
+    return laid_out(grow_blocks(value, axis), dim)
 
 
 def transpose_terms(blocks, row_hot, col_hot, everyone):
@@ -60,7 +81,7 @@
     rates = sigma[0][:, None]
     needed = demand[0]
     for step in range(ITERS):
-        everyone = lax.all_gather(dual.astype(jnp.bfloat16), "col", axis=0, tiled=True).reshape(
+        everyone = gather_by_bits(dual.astype(jnp.bfloat16), "col", 0).reshape(
             groups, width, scenarios
         )
         per_col = transpose_terms(blocks, row_hot, col_hot, everyone)

time: 187 us -> 151 us (0.81)
  blocking collectives: 127 us -> 44.1 us
  waiting for transfers between devices: 29.5 us -> 61.4 us
  starting transfers between devices: 0.08 us -> 15.4 us
    all_gather x2 -> x0, blocking collectives: 83.2 us -> none  [on_device(): lax.all_gather(dual.astype(jnp.bfloat16), 'col', axis=0, tiled=True)]
    ppermute x0 -> x8, waiting for transfers between devices: none -> 24.4 us  [grow_blocks(): other = lax.ppermute(pieces, axis, [(i, i ^ bit) for i in range(peers)])]
    ppermute x0 -> x8, starting transfers between devices: none -> 15.3 us  [grow_blocks(): other = lax.ppermute(pieces, axis, [(i, i ^ bit) for i in range(peers)])]
    psum x2, waiting for transfers between devices: 29.5 us -> 37 us  [on_device(): back = lax.psum(flat, 'row')]
  transfers between devices with their start and end apart: 2 -> 10, of which waited for: 2 -> 10; matrix products, arithmetic and copies ran while one was open for 0% -> 0% of each run, Pallas kernels for 0% -> 0%
where the time goes in v1:
time: 151 us
  waiting for transfers between devices  61.4 us (41%)
  blocking collectives  44.1 us (29%)
  starting transfers between devices  15.4 us (10%)
  between operations  15 us (10%)
  other arithmetic  5.71 us (4%)
  matrix products  5 us (3%)
  local copies, waits for them, and re-layouts  4.07 us (3%)
    all_to_all x2, blocking collectives, on_device(): lax.all_to_all(outgoing, 'col', split_axis=0, concat_axis=0, tiled=True)  44.1 us
    psum x2, waiting for transfers between devices, on_device(): back = lax.psum(flat, 'row')  37 us
    ppermute x8, waiting for transfers between devices, grow_blocks(): other = lax.ppermute(pieces, axis, [(i, i ^ bit) for i in range(peers)])  24.4 us
    ppermute x8, starting transfers between devices, grow_blocks(): other = lax.ppermute(pieces, axis, [(i, i ^ bit) for i in range(peers)])  15.3 us
    convert_element_type x2, other arithmetic, on_device(): (2.0 * new_primal - primal).astype(jnp.bfloat16)  3.83 us
  transfers between devices with their start and end apart: 10, of which 10 were waited for; matrix products, arithmetic and copies ran while one was open for 0% of the time, Pallas kernels for 0%

profile of v1, /device:TPU:0, one launch (start us, length us, event | category | flops | bytes accessed | tf_op | source)
XLA Modules:
  0.0 150.7 jit_solution(7057167886685637806)
XLA Ops:
  7.2 0.8 convert_element_type.34
  8.0 2.9 %collective-permute-start = (bf16[1,64,128]{2,1,0:T(8,128)(2,1)S(1)}, bf16[1,64,128]{2,1,0:T(8,128)(2,1)S(1)}, u32[]{:S(2)}, u32[]{:S(2)}) collective-permute-start(bf16[1,64,128]{2,1,0:T(8,128)(2,1)S(1)} %convert_element_type.34), channel_id=1, source_target_pairs={{0,2},{2,0},{4,6},{6,4},{8,10},{10,8},{12,14},{14,12},{16,18},{18,... | collective-permute-start | bytes 49160 | tf_op jit(solution)/shard_map/ppermute | solution.py:19
  11.0 1.7 %collective-permute-done = bf16[1,64,128]{2,1,0:T(8,128)(2,1)S(1)} collective-permute-done((bf16[1,64,128]{2,1,0:T(8,128)(2,1)S(1)}, bf16[1,64,128]{2,1,0:T(8,128)(2,1)S(1)}, u32[]{:S(2)}, u32[]{:S(2)}) %collective-permute-start) | collective-permute-done | bytes 16416 | tf_op jit(solution)/shard_map/ppermute | solution.py:19
  12.7 2.1 %collective-permute-start.1 = (bf16[2,64,128]{2,1,0:T(8,128)(2,1)S(1)}, bf16[2,64,128]{2,1,0:T(8,128)(2,1)S(1)}, u32[]{:S(2)}, u32[]{:S(2)}) collective-permute-start(bf16[2,64,128]{2,1,0:T(8,128)(2,1)S(1)} %pad_maximum_fusion.6), channel_id=1, source_target_pairs={{0,4},{2,6},{4,0},{6,2},{8,12},{10,14},{12,8},{14,10},{16,20},{18,... | collective-permute-start | bytes 98312 | tf_op jit(solution)/shard_map/ppermute | solution.py:19
  15.5 1.2 collective-permute-done.1
  16.8 2.1 %collective-permute-start.2 = (bf16[4,64,128]{2,1,0:T(8,128)(2,1)S(1)}, bf16[4,64,128]{2,1,0:T(8,128)(2,1)S(1)}, u32[]{:S(2)}, u32[]{:S(2)}) collective-permute-start(bf16[4,64,128]{2,1,0:T(8,128)(2,1)S(1)} %pad_maximum_fusion.4), channel_id=1, source_target_pairs={{0,8},{2,10},{4,12},{6,14},{8,0},{10,2},{12,4},{14,6},{16,24},{18,... | collective-permute-start | bytes 196616 | tf_op jit(solution)/shard_map/ppermute | solution.py:19
  18.9 2.2 %collective-permute-done.2 = bf16[4,64,128]{2,1,0:T(8,128)(2,1)S(1)} collective-permute-done((bf16[4,64,128]{2,1,0:T(8,128)(2,1)S(1)}, bf16[4,64,128]{2,1,0:T(8,128)(2,1)S(1)}, u32[]{:S(2)}, u32[]{:S(2)}) %collective-permute-start.2) | collective-permute-done | bytes 65568 | tf_op jit(solution)/shard_map/ppermute | solution.py:19
  21.2 3.8 %collective-permute-start.3 = (bf16[8,64,128]{2,1,0:T(8,128)(2,1)S(1)}, bf16[8,64,128]{2,1,0:T(8,128)(2,1)S(1)}, u32[]{:S(2)}, u32[]{:S(2)}) collective-permute-start(bf16[8,64,128]{2,1,0:T(8,128)(2,1)S(1)} %pad_maximum_fusion.2), channel_id=1, source_target_pairs={{0,16},{2,18},{4,20},{6,22},{8,24},{10,26},{12,28},{14,30},{16,0},... | collective-permute-start | bytes 393224 | tf_op jit(solution)/shard_map/ppermute | solution.py:19
  25.0 0.7 copy-done.9
  25.7 3.7 %collective-permute-done.3 = bf16[8,64,128]{2,1,0:T(8,128)(2,1)S(1)} collective-permute-done((bf16[8,64,128]{2,1,0:T(8,128)(2,1)S(1)}, bf16[8,64,128]{2,1,0:T(8,128)(2,1)S(1)}, u32[]{:S(2)}, u32[]{:S(2)}) %collective-permute-start.3) | collective-permute-done | bytes 131104 | tf_op jit(solution)/shard_map/ppermute | solution.py:19
  30.3 0.6 fusion.6
  30.9 0.8 copy.13
  31.8 19.7 %all-reduce.3.cloned.1.call-done = f32[1024,128]{1,0:T(8,128)} async-done(((f32[1024,128]{1,0:T(8,128)}), f32[1024,128]{1,0:T(8,128)}) %all-reduce.3.cloned.1.call-update) | async-done | bytes 524304 | tf_op jit(solution)/shard_map/psum | solution.py:89
  51.6 1.5 %subtract_convert_fusion.1 = bf16[1024,128]{1,0:T(8,128)(2,1)S(1)} fusion(f32[1024,128]{1,0:T(8,128)S(1)} %copy-done.1, f32[1024]{0:T(1024)S(1)} %copy-done.5, f32[1024,128]{1,0:T(8,128)} %all-reduce.3.cloned.1.call-done, f32[1024]{0:T(1024)S(1)} %copy-done.6, f32[1024]{0:T(1024)S(1)} %copy-done.7), kind=kLoop, calls=%fused_computation.22 | loop fusion | flops 1048576 | bytes 1323008 | tf_op jit(solution)/shard_map/convert_element_type | solution.py:94
  54.0 0.6 fusion.4
  54.7 22.1 %all_to_all.10 = f32[16,64,128]{2,1,0:T(8,128)S(1)} all-to-all(f32[16,64,128]{2,1,0:T(8,128)S(1)} %bitcast.68), channel_id=1, replica_groups=mesh['col'=16,'row'=2] {'col'}, dimensions={0} | all-to-all | bytes 1048576 | tf_op jit(solution)/shard_map/all_to_all | solution.py:98
  76.8 0.7 copy-done.4
  77.6 0.6 collective-permute-start.4
  78.2 3.2 %collective-permute-done.4 = bf16[1,64,128]{2,1,0:T(8,128)(2,1)S(1)} collective-permute-done((bf16[1,64,128]{2,1,0:T(8,128)(2,1)S(1)}, bf16[1,64,128]{2,1,0:T(8,128)(2,1)S(1)}, u32[]{:S(2)}, u32[]{:S(2)}) %collective-permute-start.4) | collective-permute-done | bytes 16416 | tf_op jit(solution)/shard_map/ppermute | solution.py:19
  81.3 1.1 collective-permute-start.5
  82.4 2.9 %collective-permute-done.5 = bf16[2,64,128]{2,1,0:T(8,128)(2,1)S(1)} collective-permute-done((bf16[2,64,128]{2,1,0:T(8,128)(2,1)S(1)}, bf16[2,64,128]{2,1,0:T(8,128)(2,1)S(1)}, u32[]{:S(2)}, u32[]{:S(2)}) %collective-permute-start.5) | collective-permute-done | bytes 32800 | tf_op jit(solution)/shard_map/ppermute | solution.py:19
  85.4 1.4 collective-permute-start.6
  86.8 3.3 %collective-permute-done.6 = bf16[4,64,128]{2,1,0:T(8,128)(2,1)S(1)} collective-permute-done((bf16[4,64,128]{2,1,0:T(8,128)(2,1)S(1)}, bf16[4,64,128]{2,1,0:T(8,128)(2,1)S(1)}, u32[]{:S(2)}, u32[]{:S(2)}) %collective-permute-start.6) | collective-permute-done | bytes 65568 | tf_op jit(solution)/shard_map/ppermute | solution.py:19
  90.1 1.2 collective-permute-start.7
  91.3 6.2 %collective-permute-done.7 = bf16[8,64,128]{2,1,0:T(8,128)(2,1)S(1)} collective-permute-done((bf16[8,64,128]{2,1,0:T(8,128)(2,1)S(1)}, bf16[8,64,128]{2,1,0:T(8,128)(2,1)S(1)}, u32[]{:S(2)}, u32[]{:S(2)}) %collective-permute-start.7) | collective-permute-done | bytes 131104 | tf_op jit(solution)/shard_map/ppermute | solution.py:19
  98.4 0.6 fusion.2
  99.0 0.8 copy.15
  99.9 17.3 %all-reduce.5.cloned.1.call-done = f32[1024,128]{1,0:T(8,128)} async-done(((f32[1024,128]{1,0:T(8,128)}), f32[1024,128]{1,0:T(8,128)}) %all-reduce.5.cloned.1.call-update) | async-done | bytes 524304 | tf_op jit(solution)/shard_map/psum | solution.py:89
  117.1 2.3 %subtract_convert_fusion = (bf16[1024,128]{1,0:T(8,128)(2,1)S(1)}, f32[1024,128]{1,0:T(8,128)}) fusion(f32[1024]{0:T(1024)S(1)} %copy-done.5, f32[1024,128]{1,0:T(8,128)S(1)} %copy-done.1, f32[1024,128]{1,0:T(8,128)S(1)} %copy-done.2, f32[1024]{0:T(1024)S(1)} %copy-done.6, f32[1024]{0:T(1024)S(1)} %copy-done.7, f32[1024,128]{1,0:T(8,128)} %all-reduce.5.cloned.1.call-done), kind=kLoop, calls=%fused_computation.20 | loop fusion | flops 1703936 | bytes 2371584 | tf_op jit(solution)/shard_map/convert_element_type | solution.py:94
  120.4 0.6 fusion
  121.0 22.1 %all_to_all.11 = f32[16,64,128]{2,1,0:T(8,128)S(1)} all-to-all(f32[16,64,128]{2,1,0:T(8,128)S(1)} %bitcast.69), channel_id=1, replica_groups=mesh['col'=16,'row'=2] {'col'}, dimensions={0} | all-to-all | bytes 1048576 | tf_op jit(solution)/shard_map/all_to_all | solution.py:98
  143.1 0.7 fusion.26
  (59 shorter events, 4.2 us)
Async XLA Ops:
  7.2 22.6 %copy-start = (bf16[1,1,4,256,256]{4,3,2,1,0:T(8,128)(2,1)S(1)}, bf16[1,1,4,256,256]{4,3,2,1,0:T(8,128)(2,1)}, u32[]{:S(2)}) copy-start(bf16[1,1,4,256,256]{4,3,2,1,0:T(8,128)(2,1)} %param.11) | copy-start | bytes 1572868
  7.2 5.5 %copy-start.3 = (f32[1,64,128]{2,1,0:T(8,128)S(1)}, f32[1,64,128]{2,1,0:T(8,128)}, u32[]{:S(2)}) copy-start(f32[1,64,128]{2,1,0:T(8,128)} %param.21) | copy-start | bytes 98308
  7.2 44.4 %all-reduce.3.cloned.1.call-start = ((), (), s32[]{:S(2)}) async-start(), calls=%async_computation.2 | async-start | bytes 1048576 | tf_op jit(solution)/shard_map/psum | solution.py:89
  8.0 4.7 %collective-permute-start = (bf16[1,64,128]{2,1,0:T(8,128)(2,1)S(1)}, bf16[1,64,128]{2,1,0:T(8,128)(2,1)S(1)}, u32[]{:S(2)}, u32[]{:S(2)}) collective-permute-start(bf16[1,64,128]{2,1,0:T(8,128)(2,1)S(1)} %convert_element_type.34), channel_id=1, source_target_pairs={{0,2},{2,0},{4,6},{6,4},{8,10},{10,8},{12,14},{14,12},{16,18},{18,... | collective-permute-start | bytes 49160 | tf_op jit(solution)/shard_map/ppermute | solution.py:19
  12.7 4.0 %collective-permute-start.1 = (bf16[2,64,128]{2,1,0:T(8,128)(2,1)S(1)}, bf16[2,64,128]{2,1,0:T(8,128)(2,1)S(1)}, u32[]{:S(2)}, u32[]{:S(2)}) collective-permute-start(bf16[2,64,128]{2,1,0:T(8,128)(2,1)S(1)} %pad_maximum_fusion.6), channel_id=1, source_target_pairs={{0,4},{2,6},{4,0},{6,2},{8,12},{10,14},{12,8},{14,10},{16,20},{18,... | collective-permute-start | bytes 98312 | tf_op jit(solution)/shard_map/ppermute | solution.py:19
  16.8 4.4 %collective-permute-start.2 = (bf16[4,64,128]{2,1,0:T(8,128)(2,1)S(1)}, bf16[4,64,128]{2,1,0:T(8,128)(2,1)S(1)}, u32[]{:S(2)}, u32[]{:S(2)}) collective-permute-start(bf16[4,64,128]{2,1,0:T(8,128)(2,1)S(1)} %pad_maximum_fusion.4), channel_id=1, source_target_pairs={{0,8},{2,10},{4,12},{6,14},{8,0},{10,2},{12,4},{14,6},{16,24},{18,... | collective-permute-start | bytes 196616 | tf_op jit(solution)/shard_map/ppermute | solution.py:19
  21.2 8.2 %collective-permute-start.3 = (bf16[8,64,128]{2,1,0:T(8,128)(2,1)S(1)}, bf16[8,64,128]{2,1,0:T(8,128)(2,1)S(1)}, u32[]{:S(2)}, u32[]{:S(2)}) collective-permute-start(bf16[8,64,128]{2,1,0:T(8,128)(2,1)S(1)} %pad_maximum_fusion.2), channel_id=1, source_target_pairs={{0,16},{2,18},{4,20},{6,22},{8,24},{10,26},{12,28},{14,30},{16,0},... | collective-permute-start | bytes 393224 | tf_op jit(solution)/shard_map/ppermute | solution.py:19
  25.0 0.7 copy-start.9
  25.0 0.7 copy-start.10
  30.9 20.6 %copy-start.6 = (f32[1024]{0:T(1024)S(1)}, f32[1024]{0:T(1024)}, u32[]{:S(2)}) copy-start(f32[1024]{0:T(1024)} %param.15) | copy-start | bytes 12292
  30.9 20.6 %copy-start.7 = (f32[1024]{0:T(1024)S(1)}, f32[1024]{0:T(1024)}, u32[]{:S(2)}) copy-start(f32[1024]{0:T(1024)} %param.17) | copy-start | bytes 12292
  31.8 19.8 %copy-start.1 = (f32[1024,128]{1,0:T(8,128)S(1)}, f32[1024,128]{1,0:T(8,128)}, u32[]{:S(2)}) copy-start(f32[1024,128]{1,0:T(8,128)} %param.20) | copy-start | bytes 1572868
  31.8 19.8 %copy-start.5 = (f32[1024]{0:T(1024)S(1)}, f32[1024]{0:T(1024)}, u32[]{:S(2)}) copy-start(f32[1024]{0:T(1024)} %param.16) | copy-start | bytes 12292
  31.8 85.3 %all-reduce.5.cloned.1.call-start = ((), (), s32[]{:S(2)}) async-start(), calls=%async_computation.3 | async-start | bytes 1048576 | tf_op jit(solution)/shard_map/psum | solution.py:89
  76.7 0.8 copy-start.4
  76.8 0.7 copy-start.8
  77.6 3.8 %collective-permute-start.4 = (bf16[1,64,128]{2,1,0:T(8,128)(2,1)S(1)}, bf16[1,64,128]{2,1,0:T(8,128)(2,1)S(1)}, u32[]{:S(2)}, u32[]{:S(2)}) collective-permute-start(bf16[1,64,128]{2,1,0:T(8,128)(2,1)S(1)} %fusion.34), channel_id=1, source_target_pairs={{0,2},{2,0},{4,6},{6,4},{8,10},{10,8},{12,14},{14,12},{16,18},{18,... | collective-permute-start | bytes 49160 | tf_op jit(solution)/shard_map/ppermute | solution.py:19
  81.3 4.0 %collective-permute-start.5 = (bf16[2,64,128]{2,1,0:T(8,128)(2,1)S(1)}, bf16[2,64,128]{2,1,0:T(8,128)(2,1)S(1)}, u32[]{:S(2)}, u32[]{:S(2)}) collective-permute-start(bf16[2,64,128]{2,1,0:T(8,128)(2,1)S(1)} %pad_maximum_fusion.7), channel_id=1, source_target_pairs={{0,4},{2,6},{4,0},{6,2},{8,12},{10,14},{12,8},{14,10},{16,20},{18,... | collective-permute-start | bytes 98312 | tf_op jit(solution)/shard_map/ppermute | solution.py:19
  85.4 4.7 %collective-permute-start.6 = (bf16[4,64,128]{2,1,0:T(8,128)(2,1)S(1)}, bf16[4,64,128]{2,1,0:T(8,128)(2,1)S(1)}, u32[]{:S(2)}, u32[]{:S(2)}) collective-permute-start(bf16[4,64,128]{2,1,0:T(8,128)(2,1)S(1)} %pad_maximum_fusion.5), channel_id=1, source_target_pairs={{0,8},{2,10},{4,12},{6,14},{8,0},{10,2},{12,4},{14,6},{16,24},{18,... | collective-permute-start | bytes 196616 | tf_op jit(solution)/shard_map/ppermute | solution.py:19
  90.1 7.3 %collective-permute-start.7 = (bf16[8,64,128]{2,1,0:T(8,128)(2,1)S(1)}, bf16[8,64,128]{2,1,0:T(8,128)(2,1)S(1)}, u32[]{:S(2)}, u32[]{:S(2)}) collective-permute-start(bf16[8,64,128]{2,1,0:T(8,128)(2,1)S(1)} %pad_maximum_fusion.3), channel_id=1, source_target_pairs={{0,16},{2,18},{4,20},{6,22},{8,24},{10,26},{12,28},{14,30},{16,0},... | collective-permute-start | bytes 393224 | tf_op jit(solution)/shard_map/ppermute | solution.py:19
  99.8 17.3 %copy-start.2 = (f32[1024,128]{1,0:T(8,128)S(1)}, f32[1024,128]{1,0:T(8,128)}, u32[]{:S(2)}) copy-start(f32[1024,128]{1,0:T(8,128)} %all-reduce.3.cloned.1.call-done) | copy-start | bytes 1572868
Sparse Core Ops, SparseCore 0:
  31.9 19.5 all-reduce.2
  100.0 17.1 all-reduce.4
